TPU v7x, 32 devices: a whole 2x2x4 slice. The times are simulated.
32 devices in a mesh: chan: 16 (over z, y, core), patch: 2 (over x).
Axes of the slice: x: 2, y: 2, z: 4, core: 2. Of those that a mesh axis runs over, the one named last changes fastest.
Arguments:
- volume: bfloat16 [2, 2048, 1024], P('patch', 'chan'), may hold values from -6 to 6
- depth_kernel: bfloat16 [27, 2048], P(None, 'chan'), may hold values from -1.25 to 1.25
- mix_weight: bfloat16 [2048, 2048], P('chan'), may hold values from -0.125 to 0.125
- mix_bias: bfloat16 [2048], P('chan'), may hold values from -3 to 3
- out_grad: bfloat16 [2, 2048, 1024], P('patch', 'chan'), may hold values from -1.5 to 1.5
Outputs:
- activated: bfloat16 [2, 2048, 1024], P('patch', 'chan')
- volume_grad: bfloat16 [2, 2048, 1024], P('patch', 'chan')
- kernel_grad: float32 [27, 2048], P(None, 'chan')
- weight_grad: float32 [2048, 2048], P('chan')
- bias_grad: float32 [2048], P('chan')
All inputs are finite; a program needn't handle non-finite values.
Results may differ from a plain program's by a relative error of at most 0.011.
Values may be sent and summed in bfloat16 or wider, within the bound.
No kernel may reach another device: no remote copies, remote signals or barrier semaphores. Data moves between devices by JAX's collectives and lax.ppermute only.
A program may use at most 64 MiB of HBM per device.

v0:
```python
import jax
import jax.numpy as jnp
from jax import lax
from jax.experimental import pallas as pl
from jax.experimental.pallas import tpu as pltpu
from jax.sharding import PartitionSpec as P

DEPTH = 2
ROWS = 16
SIDE = 32
PLANE = ROWS * SIDE
LANES = 128
VREGS = PLANE // LANES
GROUP = 8
STEP_ROWS = 16
TAPS = 27
TAP_ROWS = 32
BLOCK_ROWS = 32
MIB = 1024 * 1024


def chip_at(place, chips):
    return jnp.where(place < chips // 2, 2 * place, 2 * (chips - 1 - place) + 1)


def place_of(chip, chips):
    return jnp.where(chip % 2 == 0, chip // 2, chips - 1 - chip // 2)


def lane_index():
    return lax.broadcasted_iota(jnp.int32, (GROUP, LANES), 1)


def column_shift(tiles, step, lane):
    if step == 0:
        return tiles
    inside = lane % SIDE != (SIDE - 1 if step > 0 else 0)
    return [
        jnp.where(inside, pltpu.roll(tile, (-step) % LANES, 1), 0.0) for tile in tiles
    ]


def row_shift(tiles, step, lane):
    if step == 0:
        return tiles
    turned = [pltpu.roll(tile, (-step * SIDE) % LANES, 1) for tile in tiles]
    zero = jnp.zeros_like(tiles[0])
    if step > 0:
        ahead = turned[1:] + [zero]
        return [jnp.where(lane < LANES - SIDE, now, far) for now, far in zip(turned, ahead)]
    behind = [zero] + turned[:-1]
    return [jnp.where(lane >= SIDE, now, far) for now, far in zip(turned, behind)]


def tile_list(values):
    return [values[:, LANES * at : LANES * (at + 1)] for at in range(VREGS)]


def add_tiles(left, right):
    return right if left is None else [a + b for a, b in zip(left, right)]


def scale_tiles(column, tiles):
    wide = jnp.broadcast_to(column, (GROUP, LANES))
    return [wide * tile for tile in tiles]


def tap_columns(kernel_ref):
    taps = kernel_ref[...].astype(jnp.float32)
    core = lax.axis_index("chan") % 2
    down, same, up = taps[0:9], taps[9:18], taps[18:27]
    pad = jnp.zeros((TAP_ROWS - TAPS, taps.shape[1]), jnp.float32)
    order = [same, jnp.where(core == 0, up, down), jnp.where(core == 0, down, up), pad]
    return jnp.concatenate(order, axis=0).T


def spread_taps(kernel_ref, wide_ref):
    columns = tap_columns(kernel_ref)
    for t in range(wide_ref.shape[0]):
        wide_ref[t] = jnp.broadcast_to(columns[:, t : t + 1], (columns.shape[0], LANES))


def spread_kernel(kernel_ref, wide_ref):
    spread_taps(kernel_ref, wide_ref)


def depthwise_rows(vol_ref, wide_ref, at, core, lane):
    rows = pl.ds(at, STEP_ROWS)
    sources = [
        vol_ref[rows, pl.ds(pl.multiple_of(plane * PLANE, PLANE), PLANE)].astype(jnp.float32)
        for plane in (core, 1 - core)
    ]
    parts = []
    for low in range(0, STEP_ROWS, GROUP):
        group = pl.ds(at + low, GROUP)
        tiles = [tile_list(values[low : low + GROUP]) for values in sources]
        moved = [[column_shift(plane, c, lane) for c in (-1, 0, 1)] for plane in tiles]
        lines = [None] * 3
        for b in range(3):
            for side in range(2):
                for c in range(3):
                    wide = wide_ref[9 * side + 3 * b + c, group, :]
                    lines[b] = add_tiles(lines[b], [wide * tile for tile in moved[side][c]])
        shifted = [row_shift(lines[b], b - 1, lane) for b in (0, 2)]
        total = add_tiles(add_tiles(lines[1], shifted[0]), shifted[1])
        parts.append(jnp.concatenate(total, axis=1))
    return jnp.concatenate(parts, axis=0).astype(jnp.bfloat16)


def each_rows(m, step, unroll):
    size = min(unroll * STEP_ROWS, m)

    def run(index, carry):
        for at in range(0, size, STEP_ROWS):
            step(pl.multiple_of(index * size + at, STEP_ROWS))
        return carry

    lax.fori_loop(0, m // size, run, 0)


def depthwise_own_kernel(vol_hbm, kernel_hbm, out_ref, vol_ref, kernel_ref, wide_ref, sems):
    m = vol_ref.shape[0]
    rows = min(BLOCK_ROWS, m)
    core = lax.axis_index("chan") % 2
    lane = lane_index()
    taps_copy = pltpu.make_async_copy(kernel_hbm, kernel_ref, sems.at[0])
    taps_copy.start()
    copies = [
        pltpu.make_async_copy(
            vol_hbm.at[pl.ds(at, rows)], vol_ref.at[pl.ds(at, rows)], sems.at[1 + at // rows]
        )
        for at in range(0, m, rows)
    ]
    for copy in copies:
        copy.start()
    taps_copy.wait()
    spread_taps(kernel_ref, wide_ref)
    for block, copy in enumerate(copies):
        copy.wait()
        for at in range(block * rows, (block + 1) * rows, STEP_ROWS):
            out_ref[at : at + STEP_ROWS, :] = depthwise_rows(vol_ref, wide_ref, at, core, lane)


def depthwise_theirs_kernel(vol_ref, kernel_ref, own_ref, out_ref, wide_ref):
    m = vol_ref.shape[0]
    core = lax.axis_index("chan") % 2
    lane = lane_index()
    spread_taps(kernel_ref, wide_ref)
    out_ref[:m, :] = own_ref[...]

    def step(at):
        out_ref[pl.ds(m + at, STEP_ROWS), :] = depthwise_rows(vol_ref, wide_ref, at, core, lane)

    each_rows(m, step, 4)


VMEM_SPEC = pl.BlockSpec(memory_space=pltpu.VMEM)
HBM_SPEC = pl.BlockSpec(memory_space=pltpu.HBM)


ANY_SPEC = pl.BlockSpec(memory_space=pl.ANY)


def vmem_call(
    kernel, operands, outs, name, scratch=(), alias=None, free=(), hbm=False, out_free=()
):
    if hbm:
        operands = [pltpu.with_memory_space_constraint(x, pltpu.HBM) for x in operands]
    spec = HBM_SPEC if hbm else VMEM_SPEC
    return pl.pallas_call(
        kernel,
        out_shape=outs,
        in_specs=[ANY_SPEC if i in free else spec for i in range(len(operands))],
        out_specs=[HBM_SPEC if i in out_free else VMEM_SPEC for i in range(len(outs))],
        scratch_shapes=list(scratch),
        input_output_aliases=alias or {},
        compiler_params=pltpu.CompilerParams(vmem_limit_bytes=12 * MIB),
        name=name,
    )(*operands)


def held(values):
    return pltpu.with_memory_space_constraint(values, pltpu.HBM)


def position(chips):
    index = lax.axis_index("chan")
    return index % 2, index // 2, place_of(index // 2, chips)


def turn_kernel(mine, theirs, straight, turned):
    m = mine.shape[0]
    straight[:m, :] = mine[...]
    straight[m:, :] = theirs[...]
    turned[:, :m] = mine[...].T
    turned[:, m:] = theirs[...].T


def product(weights, block):
    return jnp.dot(weights, block, preferred_element_type=jnp.float32)


def stash(piece, low, all_ref, owner, core, m):
    high = low + piece.shape[0]
    for half in range(2):
        begin, end = max(low, half * m), min(high, (half + 1) * m)
        if begin >= end:
            continue
        side = core if half == 0 else 1 - core
        at = pl.multiple_of(owner * (2 * m) + side * m + (begin - half * m), STEP_ROWS)
        all_ref[pl.ds(at, end - begin), :] = piece[begin - low : end - low, :]


def assemble_kernel(chips, *refs):
    pieces = refs[: chips - 1]
    straight, total_ref, all_ref = refs[chips - 1 :]
    core, chip, place = position(chips)
    m = pieces[0].shape[0] // 2
    for number, piece in enumerate(pieces):
        distance = (number + 1) // 2
        back = chips - distance if number % 2 == 1 else distance
        owner = chip_at((place + back) % chips, chips)
        stash(piece, 0, all_ref, owner, core, m)
    opposite = chip_at((place + chips // 2) % chips, chips)
    blank = jnp.zeros((2 * m, all_ref.shape[1]), all_ref.dtype)
    all_ref[pl.ds(pl.multiple_of(opposite * (2 * m), 2 * m), 2 * m), :] = blank
    total_ref[...] = product(straight[...], all_ref[...])


def bias_column(ref):
    return jnp.broadcast_to(ref[...].astype(jnp.float32), (GROUP, ref.shape[1])).T[:, 0:1]


def weight_rows(turned, owner, whole):
    return turned[pl.ds(pl.multiple_of(owner * whole, whole), whole), :]


def mix_kernel(
    chips,
    turned,
    right,
    left,
    total_ref,
    bias_mine,
    bias_theirs,
    og_mine,
    og_theirs,
    filled,
    act_mine,
    act_theirs,
    grad_ref,
    all_ref,
    right_ref,
    left_ref,
):
    core, _, place = position(chips)
    m = og_mine.shape[0]
    cut = right.shape[0]
    opposite = chip_at((place + chips // 2) % chips, chips)
    stash(right[...], 0, all_ref, opposite, core, m)
    stash(left[...], cut, all_ref, opposite, core, m)
    block = all_ref[pl.ds(pl.multiple_of(opposite * (2 * m), 2 * m), 2 * m), :]
    sums = total_ref[...] + lax.dot_general(
        weight_rows(turned, opposite, 2 * m),
        block,
        (((0,), (0,)), ((), ())),
        preferred_element_type=jnp.float32,
    )
    here = pl.ds(pl.multiple_of(core * PLANE, PLANE), PLANE)
    for half, (bias_ref, og_ref, act_ref) in enumerate(
        ((bias_mine, og_mine, act_mine), (bias_theirs, og_theirs, act_theirs))
    ):
        rows = slice(half * m, (half + 1) * m)
        pre = sums[rows] + bias_column(bias_ref)
        gate = jax.nn.sigmoid(pre)
        act_ref[...] = (pre * gate).astype(act_ref.dtype)
        grad = og_ref[:, here].astype(jnp.float32) * gate * (1.0 + pre * (1.0 - gate))
        grad_ref[rows, :] = grad.astype(grad_ref.dtype)
    share = product(weight_rows(turned, opposite, 2 * m), grad_ref[...])
    part = right_ref.shape[0]
    right_ref[...] = share[:part].astype(right_ref.dtype)
    left_ref[...] = share[part:].astype(left_ref.dtype)


def pass_kernel(chips, distance, half, turned, grad, came, out_ref):
    _, _, place = position(chips)
    whole = grad.shape[0]
    count = came.shape[0]
    ahead = distance if half == 0 else chips - distance
    owner = chip_at((place + ahead) % chips, chips)
    share = product(weight_rows(turned, owner, whole), grad[...])
    low = 0 if half == 0 else whole - count
    for begin, end in ((0, low), (low, low + count), (low + count, whole)):
        if begin < end:
            part = share[begin:end]
            if begin == low:
                part = part + came[...].astype(jnp.float32)
            out_ref[begin:end, :] = part.astype(out_ref.dtype)


def last_kernel(chips, turned, grad, right, left, made, summed, mine_ref, theirs_ref):
    core, chip, _ = position(chips)
    m = mine_ref.shape[0]
    total = (
        product(weight_rows(turned, chip, 2 * m), grad[...])
        + right[...].astype(jnp.float32)
        + left[...].astype(jnp.float32)
    )
    mine_ref[...] = jnp.where(core == 0, total[:m], total[m:]).astype(mine_ref.dtype)
    theirs_ref[...] = jnp.where(core == 0, total[m:], total[:m]).astype(theirs_ref.dtype)


def join_kernel(mine, theirs, out_ref):
    core = lax.axis_index("chan") % 2
    for ref, plane in ((mine, core), (theirs, 1 - core)):
        out_ref[:, pl.ds(pl.multiple_of(plane * PLANE, PLANE), PLANE)] = ref[...]


LANE_PAIRS = (((1,), (1,)), ((), ()))


def weight_theirs_kernel(grad, all_ref, out_ref, bias_ref):
    m = out_ref.shape[0]
    out_ref[...] = lax.dot_general(
        grad[m:, :], all_ref[...], LANE_PAIRS, preferred_element_type=jnp.float32
    ).astype(out_ref.dtype)
    ones = jnp.ones((GROUP, PLANE), grad.dtype)
    bias_ref[...] = lax.dot_general(
        ones, grad[...], LANE_PAIRS, preferred_element_type=jnp.float32
    )


def weight_mine_kernel(grad, all_ref, came, out_ref):
    m = out_ref.shape[0]
    total = lax.dot_general(
        grad[:m, :], all_ref[...], LANE_PAIRS, preferred_element_type=jnp.float32
    )
    out_ref[...] = (total + came[...].astype(jnp.float32)).astype(out_ref.dtype)


def plane_order(core, chunks, planes):
    planes[core] = chunks[0][...]
    planes[1 - core] = chunks[1][...]


def tap_grad_kernel(near_ref, far_ref, vol_ref, spread, out_ref, planes, sums):
    m = vol_ref.shape[0]
    lane = lane_index()
    plane_order(lax.axis_index("chan") % 2, (near_ref, far_ref), planes)

    def group(at):
        rows = pl.ds(at, STEP_ROWS)
        vol = [
            vol_ref[rows, z * PLANE : (z + 1) * PLANE].astype(jnp.float32) for z in range(DEPTH)
        ]
        grad = [planes[z, rows, :].astype(jnp.float32) for z in range(DEPTH)]
        sum_parts = []
        for low in range(0, STEP_ROWS, GROUP):
            moved_vol = [
                [column_shift(tile_list(vol[z][low : low + GROUP]), c, lane) for c in (-1, 0, 1)]
                for z in range(DEPTH)
            ]
            moved_grad = [
                [row_shift(tile_list(grad[z][low : low + GROUP]), -b, lane) for b in (-1, 0, 1)]
                for z in range(DEPTH)
            ]
            collected = jnp.zeros((GROUP, LANES), jnp.float32)
            for a in (-1, 0, 1):
                for b in range(3):
                    for c in range(3):
                        t = 9 * (a + 1) + 3 * b + c
                        acc = None
                        for z in range(DEPTH):
                            if not 0 <= z + a < DEPTH:
                                continue
                            for left, right in zip(moved_grad[z][b], moved_vol[z + a][c]):
                                acc = left * right if acc is None else acc + left * right
                        collected = jnp.where(
                            lane == t, jnp.sum(acc, axis=1, keepdims=True), collected
                        )
            sum_parts.append(collected)
        sums[rows, :] = jnp.concatenate(sum_parts, axis=0)

    each_rows(m, group, 1)
    out_ref[...] = sums[...].T[:TAPS, :]

def volume_grad_kernel(together, near_ref, far_ref, wide_ref, *refs):
    if together:
        weight_mine, weight_came, out_ref, weight_out, weight_wide, sems = refs
    else:
        (out_ref,) = refs
    m = out_ref.shape[0]
    core = lax.axis_index("chan") % 2
    lane = lane_index()

    def weight_copy(number):
        rows = pl.ds(pl.multiple_of(number * STEP_ROWS, STEP_ROWS), STEP_ROWS)
        return pltpu.make_async_copy(weight_wide.at[rows], weight_out.at[rows], sems.at[number])

    def step(at):
        rows = pl.ds(at, STEP_ROWS)
        grads = [ref[rows, :].astype(jnp.float32) for ref in (near_ref, far_ref)]
        parts = [[], []]
        for low in range(0, STEP_ROWS, GROUP):
            group = pl.ds(at + low, GROUP)
            tiles = [tile_list(values[low : low + GROUP]) for values in grads]
            moved = [[row_shift(plane, 1 - b, lane) for b in range(3)] for plane in tiles]
            for p in range(2):
                columns = [None] * 3
                for c in range(3):
                    for b in range(3):
                        t = 3 * b + c
                        columns[c] = add_tiles(
                            columns[c], [wide_ref[t, group, :] * x for x in moved[p][b]]
                        )
                        u = 9 * (2 - p) + t
                        columns[c] = add_tiles(
                            columns[c], [wide_ref[u, group, :] * x for x in moved[1 - p][b]]
                        )
                shifted = [column_shift(columns[c], 1 - c, lane) for c in (0, 2)]
                total = add_tiles(add_tiles(columns[1], shifted[0]), shifted[1])
                parts[p].append(jnp.concatenate(total, axis=1))
        for p, plane in enumerate((core, 1 - core)):
            place = pl.multiple_of(plane * PLANE, PLANE)
            out_ref[rows, pl.ds(place, PLANE)] = jnp.concatenate(parts[p], axis=0).astype(
                out_ref.dtype
            )

        if together:
            weight_wide[rows, :] = weight_mine[rows, :].astype(jnp.float32) + weight_came[
                rows, :
            ].astype(jnp.float32)
            weight_copy(at // STEP_ROWS).start()

    each_rows(m, step, 2)
    if together:
        for number in range(m // STEP_ROWS):
            weight_copy(number).wait()


def body(volume, depth_kernel, mix_weight, mix_bias, out_grad):
    n = lax.axis_size("chan")
    patches = lax.axis_size("patch")
    chips = n // 2
    half_ring = chips // 2
    core = lax.axis_index("chan") % 2
    m, channels = mix_weight.shape
    whole = 2 * m

    ring = [2 * k if k < half_ring else 2 * (chips - 1 - k) + 1 for k in range(chips)]
    to_core = [(i, i ^ 1) for i in range(n)]
    to_right = [
        (2 * ring[k] + c, 2 * ring[(k + 1) % chips] + c) for k in range(chips) for c in range(2)
    ]
    to_left = [(target, source) for source, target in to_right]

    def shape(rows, columns, kind=jnp.bfloat16):
        return jax.ShapeDtypeStruct((rows, columns), kind)

    def swap(values):
        return lax.ppermute(values, "chan", to_core)

    def send(right, left):
        return lax.ppermute(right, "chan", to_right), lax.ppermute(left, "chan", to_left)

    def over_patches(values):
        if patches != 2:
            return lax.psum(values.astype(jnp.float32), "patch")
        came = lax.ppermute(values, "patch", [(0, 1), (1, 0)])
        return values.astype(jnp.float32) + came.astype(jnp.float32)

    block_rows = min(BLOCK_ROWS, m)
    vol_mine = volume[0]
    vol_theirs = swap(vol_mine)
    kernel_theirs = swap(depth_kernel)
    wide_scratch = pltpu.VMEM((2 * TAPS // 3, m, LANES), jnp.float32)
    (mixed_own,) = vmem_call(
        depthwise_own_kernel,
        (vol_mine, depth_kernel),
        (shape(m, PLANE),),
        "depthwise_own",
        scratch=(
            pltpu.VMEM(vol_mine.shape, jnp.bfloat16),
            pltpu.VMEM(depth_kernel.shape, jnp.bfloat16),
            wide_scratch,
            pltpu.SemaphoreType.DMA((1 + m // block_rows,)),
        ),
        hbm=True,
    )
    (mixed_in,) = vmem_call(
        depthwise_theirs_kernel,
        (vol_theirs, kernel_theirs, mixed_own),
        (shape(whole, PLANE),),
        "depthwise_theirs",
        scratch=(wide_scratch,),
    )

    bias_mine = mix_bias[None, :]
    bias_theirs = swap(bias_mine)
    og_mine = out_grad[0]
    og_theirs = swap(og_mine)
    straight, turned = vmem_call(
        turn_kernel,
        (mix_weight, swap(mix_weight)),
        (shape(whole, channels), shape(channels, whole)),
        "turn",
    )

    (wide_taps,) = vmem_call(
        spread_kernel,
        (depth_kernel,),
        (jax.ShapeDtypeStruct((TAPS, m, LANES), jnp.float32),),
        "spread",
    )

    all_shape = shape(channels, PLANE)
    cut = m
    part = m
    right = left = mixed_in
    pieces = [mixed_in]
    for step in range(1, half_ring):
        right, left = send(right, left)
        pieces += [right, left]
    right, left = send(right[:cut], left[cut:])
    total, all_mixed = vmem_call(
        lambda *refs: assemble_kernel(chips, *refs),
        (*pieces, straight),
        (shape(whole, PLANE, jnp.float32), all_shape),
        "assemble",
    )
    act_mine, act_theirs, pre_grad, all_mixed, right, left = vmem_call(
        lambda *refs: mix_kernel(chips, *refs),
        (
            turned,
            right,
            left,
            total,
            bias_mine,
            bias_theirs,
            og_mine,
            og_theirs,
            all_mixed,
        ),
        (
            shape(m, PLANE),
            shape(m, PLANE),
            shape(whole, PLANE),
            all_shape,
            shape(part, PLANE),
            shape(whole - part, PLANE),
        ),
        "mix",
        alias={8: 3},
    )

    weight_shape = shape(m, channels)
    weight_theirs, bias_part = vmem_call(
        weight_theirs_kernel,
        (pre_grad, all_mixed),
        (weight_shape, shape(GROUP, whole, jnp.float32)),
        "weight_theirs",
    )
    weight_far = swap(weight_theirs)
    bias_grad = over_patches(bias_part[0, :m] + swap(bias_part[0, m:]))
    act_far = swap(act_theirs)
    (weight_sum,) = vmem_call(
        weight_mine_kernel, (pre_grad, all_mixed, weight_far), (weight_shape,), "weight_mine"
    )
    together = patches == 2
    if together:
        weight_came = lax.ppermute(weight_sum, "patch", [(0, 1), (1, 0)])
    else:
        weight_grad = over_patches(weight_sum)
    (activated,) = vmem_call(
        join_kernel, (act_mine, act_far), (shape(m, DEPTH * PLANE),), "join"
    )
    for step in range(1, half_ring):
        right, left = [
            vmem_call(
                lambda *refs, step=step, half=half: pass_kernel(
                    chips, half_ring - step, half, *refs
                ),
                (turned, pre_grad, came),
                (shape(whole, PLANE),),
                "pass",
            )[0]
            for half, came in enumerate(send(right, left))
        ]
    right, left = send(right, left)
    mine, theirs = vmem_call(
        lambda *refs: last_kernel(chips, *refs),
        (turned, pre_grad, right, left, held(activated), held(bias_grad)),
        (shape(m, PLANE),) * 2,
        "last",
        free=(4, 5),
    )
    far = swap(theirs)

    (kernel_grad,) = vmem_call(
        tap_grad_kernel,
        (mine, far, vol_mine, wide_taps),
        (shape(TAPS, m, jnp.float32),),
        "tap_grad",
        scratch=(
            pltpu.VMEM((DEPTH, m, PLANE), jnp.bfloat16),
            pltpu.VMEM((m, LANES), jnp.float32),
        ),
        free=(3,),
    )
    kernel_grad = over_patches(kernel_grad)
    weights, weight_outs, weight_scratch = (), (), ()
    if together:
        weights = (weight_sum, weight_came)
        weight_outs = (shape(m, channels, jnp.float32),)
        weight_scratch = (
            pltpu.VMEM((m, channels), jnp.float32),
            pltpu.SemaphoreType.DMA((m // STEP_ROWS,)),
        )
    volume_grad, *weight_made = vmem_call(
        lambda *refs: volume_grad_kernel(together, *refs),
        (mine, far, wide_taps, *weights),
        (shape(m, DEPTH * PLANE), *weight_outs),
        "volume_grad",
        scratch=weight_scratch,
        out_free=(1,),
    )
    if together:
        (weight_grad,) = weight_made
    return (
        activated[None],
        volume_grad[None],
        kernel_grad,
        weight_grad,
        bias_grad,
    )


def solution(mesh):
    placed = (
        P("patch", "chan", None),
        P(None, "chan"),
        P("chan", None),
        P("chan"),
        P("patch", "chan", None),
    )
    return jax.shard_map(
        body,
        mesh=mesh,
        in_specs=placed,
        out_specs=(
            P("patch", "chan", None),
            P("patch", "chan", None),
            P(None, "chan"),
            P("chan", None),
            P("chan"),
        ),
        check_vma=False,
    )
```

profile of v0, /device:TPU:0, one launch (start us, length us, event | category | flops | bytes accessed | tf_op | source)
XLA Modules:
  0.0 71.5 jit_solution(13668058484692756695)
XLA Ops:
  1.2 2.0 %depthwise_own.1.own_ref = bf16[128,512]{1,0:T(8,128)(2,1)S(1)} custom-call(bf16[128,1024]{1,0:T(8,128)(2,1)} %bitcast.10, bf16[27,128]{1,0:T(8,128)(2,1)} %kernel_ref.1), custom_call_target="tpu_custom_call" | custom-call | tf_op jit(solution)/shard_map/depthwise_own/pallas_call | solution.py:170
  3.3 1.1 %depthwise_theirs.1.refs_0_ = bf16[256,512]{1,0:T(8,128)(2,1)S(1)} custom-call(bf16[128,1024]{1,0:T(8,128)(2,1)S(1)} %collective-permute-done.1.vol_ref, bf16[27,128]{1,0:T(8,128)(2,1)S(1)} %collective-permute-done.2.kernel_ref, bf16[128,512]{1,0:T(8,128)(2,1)S(1)} %depthwise_own.1.own_ref), custom_call_target="tpu_custom_call" | custom-call | tf_op jit(solution)/shard_map/depthwise_theirs/pallas_call | solution.py:170
  4.4 3.0 %collective-permute-start.7 = (bf16[256,512]{1,0:T(8,128)(2,1)S(1)}, bf16[256,512]{1,0:T(8,128)(2,1)S(1)}, u32[]{:S(2)}, u32[]{:S(2)}) collective-permute-start(bf16[256,512]{1,0:T(8,128)(2,1)S(1)} %depthwise_theirs.1.refs_0_), channel_id=1, source_target_pairs={{8,0},{10,2},{16,8},{18,10},{24,16},{26,18},{28,24},{30,26},{20,28... | collective-permute-start | bytes 786440 | tf_op jit(solution)/shard_map/ppermute | solution.py:464
  7.5 6.5 %collective-permute-done.7.refs_2_ = bf16[256,512]{1,0:T(8,128)(2,1)S(1)} collective-permute-done((bf16[256,512]{1,0:T(8,128)(2,1)S(1)}, bf16[256,512]{1,0:T(8,128)(2,1)S(1)}, u32[]{:S(2)}, u32[]{:S(2)}) %collective-permute-start.7) | collective-permute-done | bytes 262176 | tf_op jit(solution)/shard_map/ppermute | solution.py:464
  14.0 1.7 %collective-permute-start.8 = (bf16[256,512]{1,0:T(8,128)(2,1)S(1)}, bf16[256,512]{1,0:T(8,128)(2,1)S(1)}, u32[]{:S(2)}, u32[]{:S(2)}) collective-permute-start(bf16[256,512]{1,0:T(8,128)(2,1)S(1)} %collective-permute-done.7.refs_2_), channel_id=1, source_target_pairs={{8,0},{10,2},{16,8},{18,10},{24,16},{26,18},{28,24},{30,26},{20,28... | collective-permute-start | bytes 786440 | tf_op jit(solution)/shard_map/ppermute | solution.py:464
  16.0 5.7 %collective-permute-done.8.refs_4_ = bf16[256,512]{1,0:T(8,128)(2,1)S(1)} collective-permute-done((bf16[256,512]{1,0:T(8,128)(2,1)S(1)}, bf16[256,512]{1,0:T(8,128)(2,1)S(1)}, u32[]{:S(2)}, u32[]{:S(2)}) %collective-permute-start.8) | collective-permute-done | bytes 262176 | tf_op jit(solution)/shard_map/ppermute | solution.py:464
  21.8 1.4 %collective-permute-start.9 = (bf16[256,512]{1,0:T(8,128)(2,1)S(1)}, bf16[256,512]{1,0:T(8,128)(2,1)S(1)}, u32[]{:S(2)}, u32[]{:S(2)}) collective-permute-start(bf16[256,512]{1,0:T(8,128)(2,1)S(1)} %collective-permute-done.8.refs_4_), channel_id=1, source_target_pairs={{8,0},{10,2},{16,8},{18,10},{24,16},{26,18},{28,24},{30,26},{20,28... | collective-permute-start | bytes 786440 | tf_op jit(solution)/shard_map/ppermute | solution.py:464
  23.8 4.8 %collective-permute-done.9.refs_6_ = bf16[256,512]{1,0:T(8,128)(2,1)S(1)} collective-permute-done((bf16[256,512]{1,0:T(8,128)(2,1)S(1)}, bf16[256,512]{1,0:T(8,128)(2,1)S(1)}, u32[]{:S(2)}, u32[]{:S(2)}) %collective-permute-start.9) | collective-permute-done | bytes 262176 | tf_op jit(solution)/shard_map/ppermute | solution.py:464
  28.7 1.1 %collective-permute-start.10 = (bf16[128,512]{1,0:T(8,128)(2,1)S(1)}, bf16[128,512]{1,0:T(8,128)(2,1)S(1)}, u32[]{:S(2)}, u32[]{:S(2)}) collective-permute-start(bf16[128,512]{1,0:T(8,128)(2,1)S(1)} %slice.17), channel_id=1, source_target_pairs={{8,0},{10,2},{16,8},{18,10},{24,16},{26,18},{28,24},{30,26},{20,28... | collective-permute-start | bytes 393224 | tf_op jit(solution)/shard_map/ppermute | solution.py:464
  29.8 1.0 %collective-permute-start.6 = (bf16[128,512]{1,0:T(8,128)(2,1)S(1)}, bf16[128,512]{1,0:T(8,128)(2,1)S(1)}, u32[]{:S(2)}, u32[]{:S(2)}) collective-permute-start(bf16[128,512]{1,0:T(8,128)(2,1)S(1)} %slice.16), channel_id=1, source_target_pairs={{0,8},{2,10},{8,16},{10,18},{16,24},{18,26},{24,28},{26,30},{28,20... | collective-permute-start | bytes 393224 | tf_op jit(solution)/shard_map/ppermute | solution.py:464
  33.7 1.1 %collective-permute-done.6.refs_1_ = bf16[128,512]{1,0:T(8,128)(2,1)S(1)} collective-permute-done((bf16[128,512]{1,0:T(8,128)(2,1)S(1)}, bf16[128,512]{1,0:T(8,128)(2,1)S(1)}, u32[]{:S(2)}, u32[]{:S(2)}) %collective-permute-start.6) | collective-permute-done | bytes 131104 | tf_op jit(solution)/shard_map/ppermute | solution.py:464
  35.5 1.6 %collective-permute-start.18 = (bf16[128,512]{1,0:T(8,128)(2,1)S(1)}, bf16[128,512]{1,0:T(8,128)(2,1)S(1)}, u32[]{:S(2)}, u32[]{:S(2)}) collective-permute-start(bf16[128,512]{1,0:T(8,128)(2,1)S(1)} %get-tuple-element.29), channel_id=1, source_target_pairs={{8,0},{10,2},{16,8},{18,10},{24,16},{26,18},{28,24},{30,26},{20,28... | collective-permute-start | bytes 393224 | tf_op jit(solution)/shard_map/ppermute | solution.py:464
  38.5 2.0 %collective-permute-done.18.refs_2_ = bf16[128,512]{1,0:T(8,128)(2,1)S(1)} collective-permute-done((bf16[128,512]{1,0:T(8,128)(2,1)S(1)}, bf16[128,512]{1,0:T(8,128)(2,1)S(1)}, u32[]{:S(2)}, u32[]{:S(2)}) %collective-permute-start.18) | collective-permute-done | bytes 131104 | tf_op jit(solution)/shard_map/ppermute | solution.py:464
  40.7 1.6 %collective-permute-start.19 = (bf16[256,512]{1,0:T(8,128)(2,1)S(1)}, bf16[256,512]{1,0:T(8,128)(2,1)S(1)}, u32[]{:S(2)}, u32[]{:S(2)}) collective-permute-start(bf16[256,512]{1,0:T(8,128)(2,1)S(1)} %pass.9), channel_id=1, source_target_pairs={{8,0},{10,2},{16,8},{18,10},{24,16},{26,18},{28,24},{30,26},{20,28... | collective-permute-start | bytes 786440 | tf_op jit(solution)/shard_map/ppermute | solution.py:464
  43.1 4.4 %collective-permute-done.19.refs_2_ = bf16[256,512]{1,0:T(8,128)(2,1)S(1)} collective-permute-done((bf16[256,512]{1,0:T(8,128)(2,1)S(1)}, bf16[256,512]{1,0:T(8,128)(2,1)S(1)}, u32[]{:S(2)}, u32[]{:S(2)}) %collective-permute-start.19) | collective-permute-done | bytes 262176 | tf_op jit(solution)/shard_map/ppermute | solution.py:464
  47.7 1.6 %collective-permute-start.20 = (bf16[256,512]{1,0:T(8,128)(2,1)S(1)}, bf16[256,512]{1,0:T(8,128)(2,1)S(1)}, u32[]{:S(2)}, u32[]{:S(2)}) collective-permute-start(bf16[256,512]{1,0:T(8,128)(2,1)S(1)} %pass.10), channel_id=1, source_target_pairs={{8,0},{10,2},{16,8},{18,10},{24,16},{26,18},{28,24},{30,26},{20,28... | collective-permute-start | bytes 786440 | tf_op jit(solution)/shard_map/ppermute | solution.py:464
  50.9 1.6 %collective-permute-start.26 = (bf16[128,2048]{1,0:T(8,128)(2,1)S(1)}, bf16[128,2048]{1,0:T(8,128)(2,1)S(1)}, u32[]{:S(2)}, u32[]{:S(2)}) collective-permute-start(bf16[128,2048]{1,0:T(8,128)(2,1)S(1)} %weight_mine.1.refs_3_), channel_id=1, source_target_pairs={{0,1},{1,0},{2,3},{3,2},{4,5},{5,4},{6,7},{7,6},{8,9},{9,8},{10,11... | collective-permute-start | bytes 1572872 | tf_op jit(solution)/shard_map/ppermute | solution.py:571
  52.4 2.3 %collective-permute-done.20.refs_2_ = bf16[256,512]{1,0:T(8,128)(2,1)S(1)} collective-permute-done((bf16[256,512]{1,0:T(8,128)(2,1)S(1)}, bf16[256,512]{1,0:T(8,128)(2,1)S(1)}, u32[]{:S(2)}, u32[]{:S(2)}) %collective-permute-start.20) | collective-permute-done | bytes 262176 | tf_op jit(solution)/shard_map/ppermute | solution.py:464
  55.0 1.6 %collective-permute-start.21 = (bf16[256,512]{1,0:T(8,128)(2,1)S(1)}, bf16[256,512]{1,0:T(8,128)(2,1)S(1)}, u32[]{:S(2)}, u32[]{:S(2)}) collective-permute-start(bf16[256,512]{1,0:T(8,128)(2,1)S(1)} %pass.11), channel_id=1, source_target_pairs={{8,0},{10,2},{16,8},{18,10},{24,16},{26,18},{28,24},{30,26},{20,28... | collective-permute-start | bytes 786440 | tf_op jit(solution)/shard_map/ppermute | solution.py:464
  58.5 1.5 %collective-permute-start.23 = (f32[128]{0:T(128)S(1)}, f32[128]{0:T(128)S(1)}, u32[]{:S(2)}, u32[]{:S(2)}) collective-permute-start(f32[128]{0:T(128)S(1)} %bitcast_add_fusion), channel_id=1, source_target_pairs={{0,1},{1,0},{2,3},{3,2},{4,5},{5,4},{6,7},{7,6},{8,9},{9,8},{10,11... | collective-permute-start | bytes 1544 | tf_op jit(solution)/shard_map/ppermute | solution.py:469
  60.0 2.1 %collective-permute-done.23 = f32[128]{0:T(128)S(1)} collective-permute-done((f32[128]{0:T(128)S(1)}, f32[128]{0:T(128)S(1)}, u32[]{:S(2)}, u32[]{:S(2)}) %collective-permute-start.23) | collective-permute-done | bytes 544 | tf_op jit(solution)/shard_map/ppermute | solution.py:469
  65.0 2.1 %tap_grad.1 = f32[27,128]{1,0:T(8,128)S(1)} custom-call(bf16[128,512]{1,0:T(8,128)(2,1)S(1)} %get-tuple-element.32.refs_0_.near_ref, bf16[128,512]{1,0:T(8,128)(2,1)S(1)} %collective-permute-done.24.refs_1_.far_ref, bf16[128,1024]{1,0:T(8,128)(2,1)S(1)} %bitcast.11, f32[27,128,128]{2,1,0:T(8,128)S(1)} %spread.1.refs_2_), custom_call_target="tpu_custom_call" | custom-call | tf_op jit(solution)/shard_map/tap_grad/pallas_call | solution.py:170
  67.0 1.5 %collective-permute-start.27 = (f32[27,128]{1,0:T(8,128)S(1)}, f32[27,128]{1,0:T(8,128)S(1)}, u32[]{:S(2)}, u32[]{:S(2)}) collective-permute-start(f32[27,128]{1,0:T(8,128)S(1)} %tap_grad.1), channel_id=1, source_target_pairs={{0,1},{1,0},{2,3},{3,2},{4,5},{5,4},{6,7},{7,6},{8,9},{9,8},{10,11... | collective-permute-start | bytes 41480 | tf_op jit(solution)/shard_map/ppermute | solution.py:469
  68.6 2.3 %volume_grad.1 = (bf16[128,1024]{1,0:T(8,128)(2,1)}, f32[128,2048]{1,0:T(8,128)}) custom-call(bf16[128,512]{1,0:T(8,128)(2,1)S(1)} %get-tuple-element.32.refs_0_.near_ref, bf16[128,512]{1,0:T(8,128)(2,1)S(1)} %collective-permute-done.24.refs_1_.far_ref, f32[27,128,128]{2,1,0:T(8,128)S(1)} %spread.1.refs_2_, bf16[128,2048]{1,0:T(8,128)(2,1)S(1)} %weight_mine.1.refs_3_, ...), custom_call_target="tpu_custom_call" | custom-call | tf_op jit(solution)/shard_map/volume_grad/pallas_call | solution.py:170
  (66 shorter events, 15.0 us)
Async XLA Ops:
  0.6 2.6 %collective-permute-start.1 = (bf16[128,1024]{1,0:T(8,128)(2,1)}, bf16[128,1024]{1,0:T(8,128)(2,1)S(1)}, u32[]{:S(2)}, u32[]{:S(2)}) collective-permute-start(bf16[128,1024]{1,0:T(8,128)(2,1)} %bitcast.9), channel_id=1, source_target_pairs={{0,2},{2,0},{4,6},{6,4},{8,10},{10,8},{12,14},{14,12},{16,18},{18,... | collective-permute-start | bytes 786440 | tf_op jit(solution)/shard_map/ppermute | solution.py:461
  4.4 9.6 %collective-permute-start.7 = (bf16[256,512]{1,0:T(8,128)(2,1)S(1)}, bf16[256,512]{1,0:T(8,128)(2,1)S(1)}, u32[]{:S(2)}, u32[]{:S(2)}) collective-permute-start(bf16[256,512]{1,0:T(8,128)(2,1)S(1)} %depthwise_theirs.1.refs_0_), channel_id=1, source_target_pairs={{8,0},{10,2},{16,8},{18,10},{24,16},{26,18},{28,24},{30,26},{20,28... | collective-permute-start | bytes 786440 | tf_op jit(solution)/shard_map/ppermute | solution.py:464
  7.4 8.3 %collective-permute-start.3 = (bf16[256,512]{1,0:T(8,128)(2,1)S(1)}, bf16[256,512]{1,0:T(8,128)(2,1)S(1)}, u32[]{:S(2)}, u32[]{:S(2)}) collective-permute-start(bf16[256,512]{1,0:T(8,128)(2,1)S(1)} %depthwise_theirs.1.refs_0_), channel_id=1, source_target_pairs={{0,8},{2,10},{8,16},{10,18},{16,24},{18,26},{24,28},{26,30},{28,20... | collective-permute-start | bytes 786440 | tf_op jit(solution)/shard_map/ppermute | solution.py:464
  14.0 7.8 %collective-permute-start.8 = (bf16[256,512]{1,0:T(8,128)(2,1)S(1)}, bf16[256,512]{1,0:T(8,128)(2,1)S(1)}, u32[]{:S(2)}, u32[]{:S(2)}) collective-permute-start(bf16[256,512]{1,0:T(8,128)(2,1)S(1)} %collective-permute-done.7.refs_2_), channel_id=1, source_target_pairs={{8,0},{10,2},{16,8},{18,10},{24,16},{26,18},{28,24},{30,26},{20,28... | collective-permute-start | bytes 786440 | tf_op jit(solution)/shard_map/ppermute | solution.py:464
  15.7 7.5 %collective-permute-start.4 = (bf16[256,512]{1,0:T(8,128)(2,1)S(1)}, bf16[256,512]{1,0:T(8,128)(2,1)S(1)}, u32[]{:S(2)}, u32[]{:S(2)}) collective-permute-start(bf16[256,512]{1,0:T(8,128)(2,1)S(1)} %collective-permute-done.3.refs_1_), channel_id=1, source_target_pairs={{0,8},{2,10},{8,16},{10,18},{16,24},{18,26},{24,28},{26,30},{28,20... | collective-permute-start | bytes 786440 | tf_op jit(solution)/shard_map/ppermute | solution.py:464
  16.0 14.8 %collective-permute-start = (bf16[128,2048]{1,0:T(8,128)(2,1)}, bf16[128,2048]{1,0:T(8,128)(2,1)S(1)}, u32[]{:S(2)}, u32[]{:S(2)}) collective-permute-start(bf16[128,2048]{1,0:T(8,128)(2,1)} %mine.1), channel_id=1, source_target_pairs={{0,2},{2,0},{4,6},{6,4},{8,10},{10,8},{12,14},{14,12},{16,18},{18,... | collective-permute-start | bytes 1572872 | tf_op jit(solution)/shard_map/ppermute | solution.py:461
  21.8 6.9 %collective-permute-start.9 = (bf16[256,512]{1,0:T(8,128)(2,1)S(1)}, bf16[256,512]{1,0:T(8,128)(2,1)S(1)}, u32[]{:S(2)}, u32[]{:S(2)}) collective-permute-start(bf16[256,512]{1,0:T(8,128)(2,1)S(1)} %collective-permute-done.8.refs_4_), channel_id=1, source_target_pairs={{8,0},{10,2},{16,8},{18,10},{24,16},{26,18},{28,24},{30,26},{20,28... | collective-permute-start | bytes 786440 | tf_op jit(solution)/shard_map/ppermute | solution.py:464
  23.1 6.6 %collective-permute-start.5 = (bf16[256,512]{1,0:T(8,128)(2,1)S(1)}, bf16[256,512]{1,0:T(8,128)(2,1)S(1)}, u32[]{:S(2)}, u32[]{:S(2)}) collective-permute-start(bf16[256,512]{1,0:T(8,128)(2,1)S(1)} %collective-permute-done.4.refs_3_), channel_id=1, source_target_pairs={{0,8},{2,10},{8,16},{10,18},{16,24},{18,26},{24,28},{26,30},{28,20... | collective-permute-start | bytes 786440 | tf_op jit(solution)/shard_map/ppermute | solution.py:464
  23.8 9.3 %collective-permute-start.12 = (bf16[128,1024]{1,0:T(8,128)(2,1)}, bf16[128,1024]{1,0:T(8,128)(2,1)S(1)}, u32[]{:S(2)}, u32[]{:S(2)}) collective-permute-start(bf16[128,1024]{1,0:T(8,128)(2,1)} %bitcast.12), channel_id=1, source_target_pairs={{0,2},{2,0},{4,6},{6,4},{8,10},{10,8},{12,14},{14,12},{16,18},{18,... | collective-permute-start | bytes 786440 | tf_op jit(solution)/shard_map/ppermute | solution.py:461
  28.7 5.0 %collective-permute-start.10 = (bf16[128,512]{1,0:T(8,128)(2,1)S(1)}, bf16[128,512]{1,0:T(8,128)(2,1)S(1)}, u32[]{:S(2)}, u32[]{:S(2)}) collective-permute-start(bf16[128,512]{1,0:T(8,128)(2,1)S(1)} %slice.17), channel_id=1, source_target_pairs={{8,0},{10,2},{16,8},{18,10},{24,16},{26,18},{28,24},{30,26},{20,28... | collective-permute-start | bytes 393224 | tf_op jit(solution)/shard_map/ppermute | solution.py:464
  29.8 5.0 %collective-permute-start.6 = (bf16[128,512]{1,0:T(8,128)(2,1)S(1)}, bf16[128,512]{1,0:T(8,128)(2,1)S(1)}, u32[]{:S(2)}, u32[]{:S(2)}) collective-permute-start(bf16[128,512]{1,0:T(8,128)(2,1)S(1)} %slice.16), channel_id=1, source_target_pairs={{0,8},{2,10},{8,16},{10,18},{16,24},{18,26},{24,28},{26,30},{28,20... | collective-permute-start | bytes 393224 | tf_op jit(solution)/shard_map/ppermute | solution.py:464
  35.5 5.0 %collective-permute-start.18 = (bf16[128,512]{1,0:T(8,128)(2,1)S(1)}, bf16[128,512]{1,0:T(8,128)(2,1)S(1)}, u32[]{:S(2)}, u32[]{:S(2)}) collective-permute-start(bf16[128,512]{1,0:T(8,128)(2,1)S(1)} %get-tuple-element.29), channel_id=1, source_target_pairs={{8,0},{10,2},{16,8},{18,10},{24,16},{26,18},{28,24},{30,26},{20,28... | collective-permute-start | bytes 393224 | tf_op jit(solution)/shard_map/ppermute | solution.py:464
  37.1 5.3 %collective-permute-start.14 = (bf16[128,512]{1,0:T(8,128)(2,1)S(1)}, bf16[128,512]{1,0:T(8,128)(2,1)S(1)}, u32[]{:S(2)}, u32[]{:S(2)}) collective-permute-start(bf16[128,512]{1,0:T(8,128)(2,1)S(1)} %get-tuple-element.28), channel_id=1, source_target_pairs={{0,8},{2,10},{8,16},{10,18},{16,24},{18,26},{24,28},{26,30},{28,20... | collective-permute-start | bytes 393224 | tf_op jit(solution)/shard_map/ppermute | solution.py:464
  38.4 11.6 %collective-permute-start.25 = (bf16[128,2048]{1,0:T(8,128)(2,1)S(1)}, bf16[128,2048]{1,0:T(8,128)(2,1)S(1)}, u32[]{:S(2)}, u32[]{:S(2)}) collective-permute-start(bf16[128,2048]{1,0:T(8,128)(2,1)S(1)} %get-tuple-element.34), channel_id=1, source_target_pairs={{0,2},{2,0},{4,6},{6,4},{8,10},{10,8},{12,14},{14,12},{16,18},{18,... | collective-permute-start | bytes 1572872 | tf_op jit(solution)/shard_map/ppermute | solution.py:461
  40.7 6.7 %collective-permute-start.19 = (bf16[256,512]{1,0:T(8,128)(2,1)S(1)}, bf16[256,512]{1,0:T(8,128)(2,1)S(1)}, u32[]{:S(2)}, u32[]{:S(2)}) collective-permute-start(bf16[256,512]{1,0:T(8,128)(2,1)S(1)} %pass.9), channel_id=1, source_target_pairs={{8,0},{10,2},{16,8},{18,10},{24,16},{26,18},{28,24},{30,26},{20,28... | collective-permute-start | bytes 786440 | tf_op jit(solution)/shard_map/ppermute | solution.py:464
  42.6 6.7 %collective-permute-start.15 = (bf16[256,512]{1,0:T(8,128)(2,1)S(1)}, bf16[256,512]{1,0:T(8,128)(2,1)S(1)}, u32[]{:S(2)}, u32[]{:S(2)}) collective-permute-start(bf16[256,512]{1,0:T(8,128)(2,1)S(1)} %pass.6), channel_id=1, source_target_pairs={{0,8},{2,10},{8,16},{10,18},{16,24},{18,26},{24,28},{26,30},{28,20... | collective-permute-start | bytes 786440 | tf_op jit(solution)/shard_map/ppermute | solution.py:464
  47.7 7.1 %collective-permute-start.20 = (bf16[256,512]{1,0:T(8,128)(2,1)S(1)}, bf16[256,512]{1,0:T(8,128)(2,1)S(1)}, u32[]{:S(2)}, u32[]{:S(2)}) collective-permute-start(bf16[256,512]{1,0:T(8,128)(2,1)S(1)} %pass.10), channel_id=1, source_target_pairs={{8,0},{10,2},{16,8},{18,10},{24,16},{26,18},{28,24},{30,26},{20,28... | collective-permute-start | bytes 786440 | tf_op jit(solution)/shard_map/ppermute | solution.py:464
  49.5 7.1 %collective-permute-start.16 = (bf16[256,512]{1,0:T(8,128)(2,1)S(1)}, bf16[256,512]{1,0:T(8,128)(2,1)S(1)}, u32[]{:S(2)}, u32[]{:S(2)}) collective-permute-start(bf16[256,512]{1,0:T(8,128)(2,1)S(1)} %pass.7), channel_id=1, source_target_pairs={{0,8},{2,10},{8,16},{10,18},{16,24},{18,26},{24,28},{26,30},{28,20... | collective-permute-start | bytes 786440 | tf_op jit(solution)/shard_map/ppermute | solution.py:464
  50.9 17.7 %collective-permute-start.26 = (bf16[128,2048]{1,0:T(8,128)(2,1)S(1)}, bf16[128,2048]{1,0:T(8,128)(2,1)S(1)}, u32[]{:S(2)}, u32[]{:S(2)}) collective-permute-start(bf16[128,2048]{1,0:T(8,128)(2,1)S(1)} %weight_mine.1.refs_3_), channel_id=1, source_target_pairs={{0,1},{1,0},{2,3},{3,2},{4,5},{5,4},{6,7},{7,6},{8,9},{9,8},{10,11... | collective-permute-start | bytes 1572872 | tf_op jit(solution)/shard_map/ppermute | solution.py:571
  55.0 8.3 %collective-permute-start.21 = (bf16[256,512]{1,0:T(8,128)(2,1)S(1)}, bf16[256,512]{1,0:T(8,128)(2,1)S(1)}, u32[]{:S(2)}, u32[]{:S(2)}) collective-permute-start(bf16[256,512]{1,0:T(8,128)(2,1)S(1)} %pass.11), channel_id=1, source_target_pairs={{8,0},{10,2},{16,8},{18,10},{24,16},{26,18},{28,24},{30,26},{20,28... | collective-permute-start | bytes 786440 | tf_op jit(solution)/shard_map/ppermute | solution.py:464
  56.9 6.4 %collective-permute-start.17 = (bf16[256,512]{1,0:T(8,128)(2,1)S(1)}, bf16[256,512]{1,0:T(8,128)(2,1)S(1)}, u32[]{:S(2)}, u32[]{:S(2)}) collective-permute-start(bf16[256,512]{1,0:T(8,128)(2,1)S(1)} %pass.8), channel_id=1, source_target_pairs={{0,8},{2,10},{8,16},{10,18},{16,24},{18,26},{24,28},{26,30},{28,20... | collective-permute-start | bytes 786440 | tf_op jit(solution)/shard_map/ppermute | solution.py:464
  57.4 5.2 %collective-permute-start.13 = (bf16[128,512]{1,0:T(8,128)(2,1)S(1)}, bf16[128,512]{1,0:T(8,128)(2,1)S(1)}, u32[]{:S(2)}, u32[]{:S(2)}) collective-permute-start(bf16[128,512]{1,0:T(8,128)(2,1)S(1)} %get-tuple-element.26), channel_id=1, source_target_pairs={{0,2},{2,0},{4,6},{6,4},{8,10},{10,8},{12,14},{14,12},{16,18},{18,... | collective-permute-start | bytes 393224 | tf_op jit(solution)/shard_map/ppermute | solution.py:461
  58.5 3.5 %collective-permute-start.23 = (f32[128]{0:T(128)S(1)}, f32[128]{0:T(128)S(1)}, u32[]{:S(2)}, u32[]{:S(2)}) collective-permute-start(f32[128]{0:T(128)S(1)} %bitcast_add_fusion), channel_id=1, source_target_pairs={{0,1},{1,0},{2,3},{3,2},{4,5},{5,4},{6,7},{7,6},{8,9},{9,8},{10,11... | collective-permute-start | bytes 1544 | tf_op jit(solution)/shard_map/ppermute | solution.py:469
  67.0 3.8 %collective-permute-start.27 = (f32[27,128]{1,0:T(8,128)S(1)}, f32[27,128]{1,0:T(8,128)S(1)}, u32[]{:S(2)}, u32[]{:S(2)}) collective-permute-start(f32[27,128]{1,0:T(8,128)S(1)} %tap_grad.1), channel_id=1, source_target_pairs={{0,1},{1,0},{2,3},{3,2},{4,5},{5,4},{6,7},{7,6},{8,9},{9,8},{10,11... | collective-permute-start | bytes 41480 | tf_op jit(solution)/shard_map/ppermute | solution.py:469
  (9 other events, 31.3 us)
where the time goes:
time: 71.7 us; the launch traced here: 71.5 us
  waiting for transfers between devices  31 us (43%)
  starting transfers between devices  23.6 us (33%)
  Pallas kernels  13.8 us (19%)
  other arithmetic  1.13 us (2%)
  local copies, waits for them, and re-layouts  1.08 us (2%)
  between operations  0.86 us (1%)
    ppermute x8, waiting for transfers between devices, send(): lax.ppermute(left, 'chan', to_left)  26.4 us
    pallas_call x18, Pallas kernels, vmem_call(): pl.pallas_call(kernel, out_shape=outs, in_specs=[ANY_SPEC if i in free el...  13.8 us
    ppermute x8, starting transfers between devices, send(): lax.ppermute(left, 'chan', to_left)  13.6 us
    ppermute x8, starting transfers between devices, send(): lax.ppermute(right, 'chan', to_right)  4.13 us
    ppermute x2, starting transfers between devices, over_patches(): came = lax.ppermute(values, 'patch', [(0, 1), (1, 0)])  3.02 us
    ppermute x2, waiting for transfers between devices, over_patches(): came = lax.ppermute(values, 'patch', [(0, 1), (1, 0)])  2.05 us
    ppermute x1, starting transfers between devices, body(): weight_came = lax.ppermute(weight_sum, 'patch', [(0, 1), (1, 0)])  1.55 us
    ppermute x9, waiting for transfers between devices, swap(): return lax.ppermute(values, 'chan', to_core)  1.48 us
  transfers between devices with their start and end apart: 28, of which 11 were waited for; matrix products, arithmetic and copies ran while one was open for 1% of the time, Pallas kernels for 17%

commit v1 on v0

--- a/solution.py
+++ b/solution.py
@@ -15,7 +15,7 @@
 STEP_ROWS = 16
 TAPS = 27
 TAP_ROWS = 32
-BLOCK_ROWS = 32
+BLOCK_ROWS = 64
 MIB = 1024 * 1024
 
 
@@ -298,7 +298,7 @@
             out_ref[begin:end, :] = part.astype(out_ref.dtype)
 
 
-def last_kernel(chips, turned, grad, right, left, made, summed, mine_ref, theirs_ref):
+def last_kernel(chips, turned, grad, right, left, made, mine_ref, theirs_ref):
     core, chip, _ = position(chips)
     m = mine_ref.shape[0]
     total = (
@@ -343,7 +343,9 @@
     planes[1 - core] = chunks[1][...]
 
 
-def tap_grad_kernel(near_ref, far_ref, vol_ref, spread, out_ref, planes, sums):
+def tap_grad_kernel(
+    near_ref, far_ref, vol_ref, spread, bias_ref, bias_far, out_ref, planes, sums
+):
     m = vol_ref.shape[0]
     lane = lane_index()
     plane_order(lax.axis_index("chan") % 2, (near_ref, far_ref), planes)
@@ -382,7 +384,8 @@
         sums[rows, :] = jnp.concatenate(sum_parts, axis=0)
 
     each_rows(m, group, 1)
-    out_ref[...] = sums[...].T[:TAPS, :]
+    out_ref[:TAPS, :] = sums[...].T[:TAPS, :]
+    out_ref[TAPS : TAPS + 1, :] = bias_ref[0:1, :m] + bias_far[0:1, :]
 
 def volume_grad_kernel(together, near_ref, far_ref, wide_ref, *refs):
     if together:
@@ -561,7 +564,7 @@
         "weight_theirs",
     )
     weight_far = swap(weight_theirs)
-    bias_grad = over_patches(bias_part[0, :m] + swap(bias_part[0, m:]))
+    bias_far = swap(bias_part[:, m:])
     act_far = swap(act_theirs)
     (weight_sum,) = vmem_call(
         weight_mine_kernel, (pre_grad, all_mixed, weight_far), (weight_shape,), "weight_mine"
@@ -589,17 +592,17 @@
     right, left = send(right, left)
     mine, theirs = vmem_call(
         lambda *refs: last_kernel(chips, *refs),
-        (turned, pre_grad, right, left, held(activated), held(bias_grad)),
+        (turned, pre_grad, right, left, held(activated)),
         (shape(m, PLANE),) * 2,
         "last",
-        free=(4, 5),
+        free=(4,),
     )
     far = swap(theirs)
 
     (kernel_grad,) = vmem_call(
         tap_grad_kernel,
-        (mine, far, vol_mine, wide_taps),
-        (shape(TAPS, m, jnp.float32),),
+        (mine, far, vol_mine, wide_taps, bias_part, bias_far),
+        (shape(TAPS + 1, m, jnp.float32),),
         "tap_grad",
         scratch=(
             pltpu.VMEM((DEPTH, m, PLANE), jnp.bfloat16),
@@ -607,7 +610,8 @@
         ),
         free=(3,),
     )
-    kernel_grad = over_patches(kernel_grad)
+    small_grad = over_patches(kernel_grad)
+    kernel_grad, bias_grad = small_grad[:TAPS], small_grad[TAPS]
     weights, weight_outs, weight_scratch = (), (), ()
     if together:
         weights = (weight_sum, weight_came)

time: 71.7 us -> 71.5 us (level)
  waiting for transfers between devices: 31 us -> 33.1 us
  starting transfers between devices: 23.6 us -> 22.1 us
  other arithmetic: 1.13 us -> 0.01 us
    ppermute x2 -> x1, waiting for transfers between devices: 2.05 us -> 0.01 us  [over_patches(): came = lax.ppermute(values, 'patch', [(0, 1), (1, 0)])]
    ppermute x8, waiting for transfers between devices: 26.4 us -> 28.3 us  [send(): lax.ppermute(left, 'chan', to_left)]
    ppermute x8, waiting for transfers between devices: 1.12 us -> 2.99 us  [send(): lax.ppermute(right, 'chan', to_right)]
    ppermute x2 -> x1, starting transfers between devices: 3.02 us -> 1.53 us  [over_patches(): came = lax.ppermute(values, 'patch', [(0, 1), (1, 0)])]
    add x2 -> x1, other arithmetic: 1.12 us -> 0.01 us  [over_patches(): return values.astype(jnp.float32) + came.astype(jnp.float32)]
  transfers between devices with their start and end apart: 28 -> 27, of which waited for: 11 -> 12; matrix products, arithmetic and copies ran while one was open for 1% -> 0% of each run, Pallas kernels for 17% -> 17%
where the time goes in v1:
time: 71.5 us; the launch traced here: 71.3 us
  waiting for transfers between devices  33.1 us (46%)
  starting transfers between devices  22.1 us (31%)
  Pallas kernels  13.6 us (19%)
  local copies, waits for them, and re-layouts  1.68 us (2%)
  between operations  0.88 us (1%)
    ppermute x8, waiting for transfers between devices, send(): lax.ppermute(left, 'chan', to_left)  28.3 us
    ppermute x8, starting transfers between devices, send(): lax.ppermute(left, 'chan', to_left)  13.7 us
    pallas_call x18, Pallas kernels, vmem_call(): pl.pallas_call(kernel, out_shape=outs, in_specs=[ANY_SPEC if i in free el...  13.6 us
    ppermute x8, starting transfers between devices, send(): lax.ppermute(right, 'chan', to_right)  4.12 us
    ppermute x8, waiting for transfers between devices, send(): lax.ppermute(right, 'chan', to_right)  2.99 us
    ppermute x9, waiting for transfers between devices, swap(): return lax.ppermute(values, 'chan', to_core)  1.74 us
    ppermute x1, starting transfers between devices, body(): weight_came = lax.ppermute(weight_sum, 'patch', [(0, 1), (1, 0)])  1.55 us
    ppermute x1, starting transfers between devices, over_patches(): came = lax.ppermute(values, 'patch', [(0, 1), (1, 0)])  1.53 us
  transfers between devices with their start and end apart: 27, of which 12 were waited for; matrix products, arithmetic and copies ran while one was open for 0% of the time, Pallas kernels for 17%

profile of v1, /device:TPU:0, one launch (start us, length us, event | category | flops | bytes accessed | tf_op | source)
XLA Modules:
  0.0 71.3 jit_solution(490269417039624880)
XLA Ops:
  1.2 1.8 %depthwise_own.1.own_ref = bf16[128,512]{1,0:T(8,128)(2,1)S(1)} custom-call(bf16[128,1024]{1,0:T(8,128)(2,1)} %bitcast.9, bf16[27,128]{1,0:T(8,128)(2,1)} %kernel_ref.1), custom_call_target="tpu_custom_call" | custom-call | tf_op jit(solution)/shard_map/depthwise_own/pallas_call | solution.py:170
  3.1 1.1 %depthwise_theirs.1.refs_0_ = bf16[256,512]{1,0:T(8,128)(2,1)S(1)} custom-call(bf16[128,1024]{1,0:T(8,128)(2,1)S(1)} %collective-permute-done.1.vol_ref, bf16[27,128]{1,0:T(8,128)(2,1)S(1)} %collective-permute-done.2.kernel_ref, bf16[128,512]{1,0:T(8,128)(2,1)S(1)} %depthwise_own.1.own_ref), custom_call_target="tpu_custom_call" | custom-call | tf_op jit(solution)/shard_map/depthwise_theirs/pallas_call | solution.py:170
  4.2 3.0 %collective-permute-start.7 = (bf16[256,512]{1,0:T(8,128)(2,1)S(1)}, bf16[256,512]{1,0:T(8,128)(2,1)S(1)}, u32[]{:S(2)}, u32[]{:S(2)}) collective-permute-start(bf16[256,512]{1,0:T(8,128)(2,1)S(1)} %depthwise_theirs.1.refs_0_), channel_id=1, source_target_pairs={{8,0},{10,2},{16,8},{18,10},{24,16},{26,18},{28,24},{30,26},{20,28... | collective-permute-start | bytes 786440 | tf_op jit(solution)/shard_map/ppermute | solution.py:467
  7.3 6.5 %collective-permute-done.7.refs_2_ = bf16[256,512]{1,0:T(8,128)(2,1)S(1)} collective-permute-done((bf16[256,512]{1,0:T(8,128)(2,1)S(1)}, bf16[256,512]{1,0:T(8,128)(2,1)S(1)}, u32[]{:S(2)}, u32[]{:S(2)}) %collective-permute-start.7) | collective-permute-done | bytes 262176 | tf_op jit(solution)/shard_map/ppermute | solution.py:467
  13.8 1.7 %collective-permute-start.8 = (bf16[256,512]{1,0:T(8,128)(2,1)S(1)}, bf16[256,512]{1,0:T(8,128)(2,1)S(1)}, u32[]{:S(2)}, u32[]{:S(2)}) collective-permute-start(bf16[256,512]{1,0:T(8,128)(2,1)S(1)} %collective-permute-done.7.refs_2_), channel_id=1, source_target_pairs={{8,0},{10,2},{16,8},{18,10},{24,16},{26,18},{28,24},{30,26},{20,28... | collective-permute-start | bytes 786440 | tf_op jit(solution)/shard_map/ppermute | solution.py:467
  15.9 5.7 %collective-permute-done.8.refs_4_ = bf16[256,512]{1,0:T(8,128)(2,1)S(1)} collective-permute-done((bf16[256,512]{1,0:T(8,128)(2,1)S(1)}, bf16[256,512]{1,0:T(8,128)(2,1)S(1)}, u32[]{:S(2)}, u32[]{:S(2)}) %collective-permute-start.8) | collective-permute-done | bytes 262176 | tf_op jit(solution)/shard_map/ppermute | solution.py:467
  21.6 1.4 %collective-permute-start.9 = (bf16[256,512]{1,0:T(8,128)(2,1)S(1)}, bf16[256,512]{1,0:T(8,128)(2,1)S(1)}, u32[]{:S(2)}, u32[]{:S(2)}) collective-permute-start(bf16[256,512]{1,0:T(8,128)(2,1)S(1)} %collective-permute-done.8.refs_4_), channel_id=1, source_target_pairs={{8,0},{10,2},{16,8},{18,10},{24,16},{26,18},{28,24},{30,26},{20,28... | collective-permute-start | bytes 786440 | tf_op jit(solution)/shard_map/ppermute | solution.py:467
  23.6 4.8 %collective-permute-done.9.refs_6_ = bf16[256,512]{1,0:T(8,128)(2,1)S(1)} collective-permute-done((bf16[256,512]{1,0:T(8,128)(2,1)S(1)}, bf16[256,512]{1,0:T(8,128)(2,1)S(1)}, u32[]{:S(2)}, u32[]{:S(2)}) %collective-permute-start.9) | collective-permute-done | bytes 262176 | tf_op jit(solution)/shard_map/ppermute | solution.py:467
  28.5 1.1 %collective-permute-start.10 = (bf16[128,512]{1,0:T(8,128)(2,1)S(1)}, bf16[128,512]{1,0:T(8,128)(2,1)S(1)}, u32[]{:S(2)}, u32[]{:S(2)}) collective-permute-start(bf16[128,512]{1,0:T(8,128)(2,1)S(1)} %slice.21), channel_id=1, source_target_pairs={{8,0},{10,2},{16,8},{18,10},{24,16},{26,18},{28,24},{30,26},{20,28... | collective-permute-start | bytes 393224 | tf_op jit(solution)/shard_map/ppermute | solution.py:467
  33.5 1.1 %collective-permute-done.6.refs_1_ = bf16[128,512]{1,0:T(8,128)(2,1)S(1)} collective-permute-done((bf16[128,512]{1,0:T(8,128)(2,1)S(1)}, bf16[128,512]{1,0:T(8,128)(2,1)S(1)}, u32[]{:S(2)}, u32[]{:S(2)}) %collective-permute-start.6) | collective-permute-done | bytes 131104 | tf_op jit(solution)/shard_map/ppermute | solution.py:467
  35.3 1.6 %collective-permute-start.18 = (bf16[128,512]{1,0:T(8,128)(2,1)S(1)}, bf16[128,512]{1,0:T(8,128)(2,1)S(1)}, u32[]{:S(2)}, u32[]{:S(2)}) collective-permute-start(bf16[128,512]{1,0:T(8,128)(2,1)S(1)} %get-tuple-element.29), channel_id=1, source_target_pairs={{8,0},{10,2},{16,8},{18,10},{24,16},{26,18},{28,24},{30,26},{20,28... | collective-permute-start | bytes 393224 | tf_op jit(solution)/shard_map/ppermute | solution.py:467
  38.3 2.0 %collective-permute-done.18.refs_2_ = bf16[128,512]{1,0:T(8,128)(2,1)S(1)} collective-permute-done((bf16[128,512]{1,0:T(8,128)(2,1)S(1)}, bf16[128,512]{1,0:T(8,128)(2,1)S(1)}, u32[]{:S(2)}, u32[]{:S(2)}) %collective-permute-start.18) | collective-permute-done | bytes 131104 | tf_op jit(solution)/shard_map/ppermute | solution.py:467
  40.6 1.6 %collective-permute-start.19 = (bf16[256,512]{1,0:T(8,128)(2,1)S(1)}, bf16[256,512]{1,0:T(8,128)(2,1)S(1)}, u32[]{:S(2)}, u32[]{:S(2)}) collective-permute-start(bf16[256,512]{1,0:T(8,128)(2,1)S(1)} %pass.9), channel_id=1, source_target_pairs={{8,0},{10,2},{16,8},{18,10},{24,16},{26,18},{28,24},{30,26},{20,28... | collective-permute-start | bytes 786440 | tf_op jit(solution)/shard_map/ppermute | solution.py:467
  42.9 4.4 %collective-permute-done.19.refs_2_ = bf16[256,512]{1,0:T(8,128)(2,1)S(1)} collective-permute-done((bf16[256,512]{1,0:T(8,128)(2,1)S(1)}, bf16[256,512]{1,0:T(8,128)(2,1)S(1)}, u32[]{:S(2)}, u32[]{:S(2)}) %collective-permute-start.19) | collective-permute-done | bytes 262176 | tf_op jit(solution)/shard_map/ppermute | solution.py:467
  47.5 1.6 %collective-permute-start.20 = (bf16[256,512]{1,0:T(8,128)(2,1)S(1)}, bf16[256,512]{1,0:T(8,128)(2,1)S(1)}, u32[]{:S(2)}, u32[]{:S(2)}) collective-permute-start(bf16[256,512]{1,0:T(8,128)(2,1)S(1)} %pass.10), channel_id=1, source_target_pairs={{8,0},{10,2},{16,8},{18,10},{24,16},{26,18},{28,24},{30,26},{20,28... | collective-permute-start | bytes 786440 | tf_op jit(solution)/shard_map/ppermute | solution.py:467
  50.7 1.6 %collective-permute-start.24 = (bf16[128,2048]{1,0:T(8,128)(2,1)S(1)}, bf16[128,2048]{1,0:T(8,128)(2,1)S(1)}, u32[]{:S(2)}, u32[]{:S(2)}) collective-permute-start(bf16[128,2048]{1,0:T(8,128)(2,1)S(1)} %weight_mine.1.refs_3_), channel_id=1, source_target_pairs={{0,1},{1,0},{2,3},{3,2},{4,5},{5,4},{6,7},{7,6},{8,9},{9,8},{10,11... | collective-permute-start | bytes 1572872 | tf_op jit(solution)/shard_map/ppermute | solution.py:574
  52.3 2.3 %collective-permute-done.20.refs_2_ = bf16[256,512]{1,0:T(8,128)(2,1)S(1)} collective-permute-done((bf16[256,512]{1,0:T(8,128)(2,1)S(1)}, bf16[256,512]{1,0:T(8,128)(2,1)S(1)}, u32[]{:S(2)}, u32[]{:S(2)}) %collective-permute-start.20) | collective-permute-done | bytes 262176 | tf_op jit(solution)/shard_map/ppermute | solution.py:467
  54.8 1.6 %collective-permute-start.21 = (bf16[256,512]{1,0:T(8,128)(2,1)S(1)}, bf16[256,512]{1,0:T(8,128)(2,1)S(1)}, u32[]{:S(2)}, u32[]{:S(2)}) collective-permute-start(bf16[256,512]{1,0:T(8,128)(2,1)S(1)} %pass.11), channel_id=1, source_target_pairs={{8,0},{10,2},{16,8},{18,10},{24,16},{26,18},{28,24},{30,26},{20,28... | collective-permute-start | bytes 786440 | tf_op jit(solution)/shard_map/ppermute | solution.py:467
  57.2 1.3 %collective-permute-done.13.theirs = bf16[128,512]{1,0:T(8,128)(2,1)S(1)} collective-permute-done((bf16[128,512]{1,0:T(8,128)(2,1)S(1)}, bf16[128,512]{1,0:T(8,128)(2,1)S(1)}, u32[]{:S(2)}, u32[]{:S(2)}) %collective-permute-start.13) | collective-permute-done | bytes 131104 | tf_op jit(solution)/shard_map/ppermute | solution.py:464
  59.3 2.0 %collective-permute-done.21.refs_3_ = bf16[256,512]{1,0:T(8,128)(2,1)S(1)} collective-permute-done((bf16[256,512]{1,0:T(8,128)(2,1)S(1)}, bf16[256,512]{1,0:T(8,128)(2,1)S(1)}, u32[]{:S(2)}, u32[]{:S(2)}) %collective-permute-start.21) | collective-permute-done | bytes 262176 | tf_op jit(solution)/shard_map/ppermute | solution.py:467
  61.3 1.9 %collective-permute-done.17.refs_2_ = bf16[256,512]{1,0:T(8,128)(2,1)S(1)} collective-permute-done((bf16[256,512]{1,0:T(8,128)(2,1)S(1)}, bf16[256,512]{1,0:T(8,128)(2,1)S(1)}, u32[]{:S(2)}, u32[]{:S(2)}) %collective-permute-start.17) | collective-permute-done | bytes 262176 | tf_op jit(solution)/shard_map/ppermute | solution.py:467
  64.8 2.1 %tap_grad.1 = f32[28,128]{1,0:T(8,128)S(1)} custom-call(bf16[128,512]{1,0:T(8,128)(2,1)S(1)} %get-tuple-element.30.refs_0_.near_ref, bf16[128,512]{1,0:T(8,128)(2,1)S(1)} %collective-permute-done.22.refs_1_.far_ref, bf16[128,1024]{1,0:T(8,128)(2,1)S(1)} %bitcast.10, f32[27,128,128]{2,1,0:T(8,128)S(1)} %spread.1.refs_2_, ...), custom_call_target="tpu_custom_call" | custom-call | tf_op jit(solution)/shard_map/tap_grad/pallas_call | solution.py:170
  66.9 1.5 %collective-permute-start.26 = (f32[28,128]{1,0:T(8,128)S(1)}, f32[28,128]{1,0:T(8,128)S(1)}, u32[]{:S(2)}, u32[]{:S(2)}) collective-permute-start(f32[28,128]{1,0:T(8,128)S(1)} %tap_grad.1), channel_id=1, source_target_pairs={{0,1},{1,0},{2,3},{3,2},{4,5},{5,4},{6,7},{7,6},{8,9},{9,8},{10,11... | collective-permute-start | bytes 43016 | tf_op jit(solution)/shard_map/ppermute | solution.py:472
  68.4 2.3 %volume_grad.1 = (bf16[128,1024]{1,0:T(8,128)(2,1)}, f32[128,2048]{1,0:T(8,128)}) custom-call(bf16[128,512]{1,0:T(8,128)(2,1)S(1)} %get-tuple-element.30.refs_0_.near_ref, bf16[128,512]{1,0:T(8,128)(2,1)S(1)} %collective-permute-done.22.refs_1_.far_ref, f32[27,128,128]{2,1,0:T(8,128)S(1)} %spread.1.refs_2_, bf16[128,2048]{1,0:T(8,128)(2,1)S(1)} %weight_mine.1.refs_3_, ...), custom_call_target="tpu_custom_call" | custom-call | tf_op jit(solution)/shard_map/volume_grad/pallas_call | solution.py:170
  (65 shorter events, 14.3 us)
Async XLA Ops:
  0.6 2.5 %collective-permute-start.1 = (bf16[128,1024]{1,0:T(8,128)(2,1)}, bf16[128,1024]{1,0:T(8,128)(2,1)S(1)}, u32[]{:S(2)}, u32[]{:S(2)}) collective-permute-start(bf16[128,1024]{1,0:T(8,128)(2,1)} %bitcast.8), channel_id=1, source_target_pairs={{0,2},{2,0},{4,6},{6,4},{8,10},{10,8},{12,14},{14,12},{16,18},{18,... | collective-permute-start | bytes 786440 | tf_op jit(solution)/shard_map/ppermute | solution.py:464
  1.1 1.9 %collective-permute-start.2 = (bf16[27,128]{1,0:T(8,128)(2,1)}, bf16[27,128]{1,0:T(8,128)(2,1)S(1)}, u32[]{:S(2)}, u32[]{:S(2)}) collective-permute-start(bf16[27,128]{1,0:T(8,128)(2,1)} %kernel_ref.1), channel_id=1, source_target_pairs={{0,2},{2,0},{4,6},{6,4},{8,10},{10,8},{12,14},{14,12},{16,18},{18,... | collective-permute-start | bytes 20744 | tf_op jit(solution)/shard_map/ppermute | solution.py:464
  4.2 9.6 %collective-permute-start.7 = (bf16[256,512]{1,0:T(8,128)(2,1)S(1)}, bf16[256,512]{1,0:T(8,128)(2,1)S(1)}, u32[]{:S(2)}, u32[]{:S(2)}) collective-permute-start(bf16[256,512]{1,0:T(8,128)(2,1)S(1)} %depthwise_theirs.1.refs_0_), channel_id=1, source_target_pairs={{8,0},{10,2},{16,8},{18,10},{24,16},{26,18},{28,24},{30,26},{20,28... | collective-permute-start | bytes 786440 | tf_op jit(solution)/shard_map/ppermute | solution.py:467
  7.2 8.3 %collective-permute-start.3 = (bf16[256,512]{1,0:T(8,128)(2,1)S(1)}, bf16[256,512]{1,0:T(8,128)(2,1)S(1)}, u32[]{:S(2)}, u32[]{:S(2)}) collective-permute-start(bf16[256,512]{1,0:T(8,128)(2,1)S(1)} %depthwise_theirs.1.refs_0_), channel_id=1, source_target_pairs={{0,8},{2,10},{8,16},{10,18},{16,24},{18,26},{24,28},{26,30},{28,20... | collective-permute-start | bytes 786440 | tf_op jit(solution)/shard_map/ppermute | solution.py:467
  13.8 7.8 %collective-permute-start.8 = (bf16[256,512]{1,0:T(8,128)(2,1)S(1)}, bf16[256,512]{1,0:T(8,128)(2,1)S(1)}, u32[]{:S(2)}, u32[]{:S(2)}) collective-permute-start(bf16[256,512]{1,0:T(8,128)(2,1)S(1)} %collective-permute-done.7.refs_2_), channel_id=1, source_target_pairs={{8,0},{10,2},{16,8},{18,10},{24,16},{26,18},{28,24},{30,26},{20,28... | collective-permute-start | bytes 786440 | tf_op jit(solution)/shard_map/ppermute | solution.py:467
  15.5 7.5 %collective-permute-start.4 = (bf16[256,512]{1,0:T(8,128)(2,1)S(1)}, bf16[256,512]{1,0:T(8,128)(2,1)S(1)}, u32[]{:S(2)}, u32[]{:S(2)}) collective-permute-start(bf16[256,512]{1,0:T(8,128)(2,1)S(1)} %collective-permute-done.3.refs_1_), channel_id=1, source_target_pairs={{0,8},{2,10},{8,16},{10,18},{16,24},{18,26},{24,28},{26,30},{28,20... | collective-permute-start | bytes 786440 | tf_op jit(solution)/shard_map/ppermute | solution.py:467
  15.9 14.8 %collective-permute-start = (bf16[128,2048]{1,0:T(8,128)(2,1)}, bf16[128,2048]{1,0:T(8,128)(2,1)S(1)}, u32[]{:S(2)}, u32[]{:S(2)}) collective-permute-start(bf16[128,2048]{1,0:T(8,128)(2,1)} %mine.1), channel_id=1, source_target_pairs={{0,2},{2,0},{4,6},{6,4},{8,10},{10,8},{12,14},{14,12},{16,18},{18,... | collective-permute-start | bytes 1572872 | tf_op jit(solution)/shard_map/ppermute | solution.py:464
  21.6 6.9 %collective-permute-start.9 = (bf16[256,512]{1,0:T(8,128)(2,1)S(1)}, bf16[256,512]{1,0:T(8,128)(2,1)S(1)}, u32[]{:S(2)}, u32[]{:S(2)}) collective-permute-start(bf16[256,512]{1,0:T(8,128)(2,1)S(1)} %collective-permute-done.8.refs_4_), channel_id=1, source_target_pairs={{8,0},{10,2},{16,8},{18,10},{24,16},{26,18},{28,24},{30,26},{20,28... | collective-permute-start | bytes 786440 | tf_op jit(solution)/shard_map/ppermute | solution.py:467
  23.0 6.6 %collective-permute-start.5 = (bf16[256,512]{1,0:T(8,128)(2,1)S(1)}, bf16[256,512]{1,0:T(8,128)(2,1)S(1)}, u32[]{:S(2)}, u32[]{:S(2)}) collective-permute-start(bf16[256,512]{1,0:T(8,128)(2,1)S(1)} %collective-permute-done.4.refs_3_), channel_id=1, source_target_pairs={{0,8},{2,10},{8,16},{10,18},{16,24},{18,26},{24,28},{26,30},{28,20... | collective-permute-start | bytes 786440 | tf_op jit(solution)/shard_map/ppermute | solution.py:467
  23.6 9.3 %collective-permute-start.12 = (bf16[128,1024]{1,0:T(8,128)(2,1)}, bf16[128,1024]{1,0:T(8,128)(2,1)S(1)}, u32[]{:S(2)}, u32[]{:S(2)}) collective-permute-start(bf16[128,1024]{1,0:T(8,128)(2,1)} %bitcast.11), channel_id=1, source_target_pairs={{0,2},{2,0},{4,6},{6,4},{8,10},{10,8},{12,14},{14,12},{16,18},{18,... | collective-permute-start | bytes 786440 | tf_op jit(solution)/shard_map/ppermute | solution.py:464
  28.5 5.0 %collective-permute-start.10 = (bf16[128,512]{1,0:T(8,128)(2,1)S(1)}, bf16[128,512]{1,0:T(8,128)(2,1)S(1)}, u32[]{:S(2)}, u32[]{:S(2)}) collective-permute-start(bf16[128,512]{1,0:T(8,128)(2,1)S(1)} %slice.21), channel_id=1, source_target_pairs={{8,0},{10,2},{16,8},{18,10},{24,16},{26,18},{28,24},{30,26},{20,28... | collective-permute-start | bytes 393224 | tf_op jit(solution)/shard_map/ppermute | solution.py:467
  29.6 5.0 %collective-permute-start.6 = (bf16[128,512]{1,0:T(8,128)(2,1)S(1)}, bf16[128,512]{1,0:T(8,128)(2,1)S(1)}, u32[]{:S(2)}, u32[]{:S(2)}) collective-permute-start(bf16[128,512]{1,0:T(8,128)(2,1)S(1)} %slice.20), channel_id=1, source_target_pairs={{0,8},{2,10},{8,16},{10,18},{16,24},{18,26},{24,28},{26,30},{28,20... | collective-permute-start | bytes 393224 | tf_op jit(solution)/shard_map/ppermute | solution.py:467
  30.6 2.3 %collective-permute-start.11 = (bf16[1,128]{1,0:T(2,128)(2,1)}, bf16[1,128]{1,0:T(2,128)(2,1)S(1)}, u32[]{:S(2)}, u32[]{:S(2)}) collective-permute-start(bf16[1,128]{1,0:T(2,128)(2,1)} %bitcast.13), channel_id=1, source_target_pairs={{0,2},{2,0},{4,6},{6,4},{8,10},{10,8},{12,14},{14,12},{16,18},{18,... | collective-permute-start | bytes 776 | tf_op jit(solution)/shard_map/ppermute | solution.py:464
  35.3 5.0 %collective-permute-start.18 = (bf16[128,512]{1,0:T(8,128)(2,1)S(1)}, bf16[128,512]{1,0:T(8,128)(2,1)S(1)}, u32[]{:S(2)}, u32[]{:S(2)}) collective-permute-start(bf16[128,512]{1,0:T(8,128)(2,1)S(1)} %get-tuple-element.29), channel_id=1, source_target_pairs={{8,0},{10,2},{16,8},{18,10},{24,16},{26,18},{28,24},{30,26},{20,28... | collective-permute-start | bytes 393224 | tf_op jit(solution)/shard_map/ppermute | solution.py:467
  36.9 5.3 %collective-permute-start.14 = (bf16[128,512]{1,0:T(8,128)(2,1)S(1)}, bf16[128,512]{1,0:T(8,128)(2,1)S(1)}, u32[]{:S(2)}, u32[]{:S(2)}) collective-permute-start(bf16[128,512]{1,0:T(8,128)(2,1)S(1)} %get-tuple-element.28), channel_id=1, source_target_pairs={{0,8},{2,10},{8,16},{10,18},{16,24},{18,26},{24,28},{26,30},{28,20... | collective-permute-start | bytes 393224 | tf_op jit(solution)/shard_map/ppermute | solution.py:467
  38.2 11.6 %collective-permute-start.23 = (bf16[128,2048]{1,0:T(8,128)(2,1)S(1)}, bf16[128,2048]{1,0:T(8,128)(2,1)S(1)}, u32[]{:S(2)}, u32[]{:S(2)}) collective-permute-start(bf16[128,2048]{1,0:T(8,128)(2,1)S(1)} %get-tuple-element.33), channel_id=1, source_target_pairs={{0,2},{2,0},{4,6},{6,4},{8,10},{10,8},{12,14},{14,12},{16,18},{18,... | collective-permute-start | bytes 1572872 | tf_op jit(solution)/shard_map/ppermute | solution.py:464
  40.6 6.7 %collective-permute-start.19 = (bf16[256,512]{1,0:T(8,128)(2,1)S(1)}, bf16[256,512]{1,0:T(8,128)(2,1)S(1)}, u32[]{:S(2)}, u32[]{:S(2)}) collective-permute-start(bf16[256,512]{1,0:T(8,128)(2,1)S(1)} %pass.9), channel_id=1, source_target_pairs={{8,0},{10,2},{16,8},{18,10},{24,16},{26,18},{28,24},{30,26},{20,28... | collective-permute-start | bytes 786440 | tf_op jit(solution)/shard_map/ppermute | solution.py:467
  42.4 6.7 %collective-permute-start.15 = (bf16[256,512]{1,0:T(8,128)(2,1)S(1)}, bf16[256,512]{1,0:T(8,128)(2,1)S(1)}, u32[]{:S(2)}, u32[]{:S(2)}) collective-permute-start(bf16[256,512]{1,0:T(8,128)(2,1)S(1)} %pass.6), channel_id=1, source_target_pairs={{0,8},{2,10},{8,16},{10,18},{16,24},{18,26},{24,28},{26,30},{28,20... | collective-permute-start | bytes 786440 | tf_op jit(solution)/shard_map/ppermute | solution.py:467
  47.5 7.1 %collective-permute-start.20 = (bf16[256,512]{1,0:T(8,128)(2,1)S(1)}, bf16[256,512]{1,0:T(8,128)(2,1)S(1)}, u32[]{:S(2)}, u32[]{:S(2)}) collective-permute-start(bf16[256,512]{1,0:T(8,128)(2,1)S(1)} %pass.10), channel_id=1, source_target_pairs={{8,0},{10,2},{16,8},{18,10},{24,16},{26,18},{28,24},{30,26},{20,28... | collective-permute-start | bytes 786440 | tf_op jit(solution)/shard_map/ppermute | solution.py:467
  49.4 7.1 %collective-permute-start.16 = (bf16[256,512]{1,0:T(8,128)(2,1)S(1)}, bf16[256,512]{1,0:T(8,128)(2,1)S(1)}, u32[]{:S(2)}, u32[]{:S(2)}) collective-permute-start(bf16[256,512]{1,0:T(8,128)(2,1)S(1)} %pass.7), channel_id=1, source_target_pairs={{0,8},{2,10},{8,16},{10,18},{16,24},{18,26},{24,28},{26,30},{28,20... | collective-permute-start | bytes 786440 | tf_op jit(solution)/shard_map/ppermute | solution.py:467
  50.7 17.7 %collective-permute-start.24 = (bf16[128,2048]{1,0:T(8,128)(2,1)S(1)}, bf16[128,2048]{1,0:T(8,128)(2,1)S(1)}, u32[]{:S(2)}, u32[]{:S(2)}) collective-permute-start(bf16[128,2048]{1,0:T(8,128)(2,1)S(1)} %weight_mine.1.refs_3_), channel_id=1, source_target_pairs={{0,1},{1,0},{2,3},{3,2},{4,5},{5,4},{6,7},{7,6},{8,9},{9,8},{10,11... | collective-permute-start | bytes 1572872 | tf_op jit(solution)/shard_map/ppermute | solution.py:574
  54.8 6.4 %collective-permute-start.21 = (bf16[256,512]{1,0:T(8,128)(2,1)S(1)}, bf16[256,512]{1,0:T(8,128)(2,1)S(1)}, u32[]{:S(2)}, u32[]{:S(2)}) collective-permute-start(bf16[256,512]{1,0:T(8,128)(2,1)S(1)} %pass.11), channel_id=1, source_target_pairs={{8,0},{10,2},{16,8},{18,10},{24,16},{26,18},{28,24},{30,26},{20,28... | collective-permute-start | bytes 786440 | tf_op jit(solution)/shard_map/ppermute | solution.py:467
  56.7 6.4 %collective-permute-start.17 = (bf16[256,512]{1,0:T(8,128)(2,1)S(1)}, bf16[256,512]{1,0:T(8,128)(2,1)S(1)}, u32[]{:S(2)}, u32[]{:S(2)}) collective-permute-start(bf16[256,512]{1,0:T(8,128)(2,1)S(1)} %pass.8), channel_id=1, source_target_pairs={{0,8},{2,10},{8,16},{10,18},{16,24},{18,26},{24,28},{26,30},{28,20... | collective-permute-start | bytes 786440 | tf_op jit(solution)/shard_map/ppermute | solution.py:467
  66.9 3.8 %collective-permute-start.26 = (f32[28,128]{1,0:T(8,128)S(1)}, f32[28,128]{1,0:T(8,128)S(1)}, u32[]{:S(2)}, u32[]{:S(2)}) collective-permute-start(f32[28,128]{1,0:T(8,128)S(1)} %tap_grad.1), channel_id=1, source_target_pairs={{0,1},{1,0},{2,3},{3,2},{4,5},{5,4},{6,7},{7,6},{8,9},{9,8},{10,11... | collective-permute-start | bytes 43016 | tf_op jit(solution)/shard_map/ppermute | solution.py:472
  (9 other events, 33.5 us)
